TPU v7x, 32 devices: a whole 2x2x4 slice. The times are simulated.
32 devices in a mesh: inp: 16 (over z, x, core), chan: 2 (over y).
Axes of the slice: x: 2, y: 2, z: 4, core: 2. Of those that a mesh axis runs over, the one named last changes fastest.
Arguments:
- voltages: bfloat16 [2, 4, 1024, 2048], P(None, None, ('inp', 'chan')), may hold values from -32 to 32
- positions: float32 [1024, 2], replicated, may hold values from -8 to 8
- directions: float32 [1024, 2], replicated, may hold values from -0.5 to 0.5
- basis: float32 [2, 4, 16, 1024], P(None, 'chan', None, 'inp'), may hold values from -6 to 6
- rank_count: int32 [4], P('chan'), may hold values from 1 to 16, as said below
Outputs:
- beam_power: float32 [1024, 4, 128], P('inp', 'chan')
Inputs may be any that keep to these rules, and one draw needn't show every extreme that they name: `rank_count`: each channel uses at least one basis vector, and some channel uses all 16.
All inputs are finite; a program needn't handle non-finite values.
Results may differ from a plain program's by a relative error of at most 0.0023.
Values may be sent and summed in bfloat16 or wider, within the bound.
A program may use at most 64 MiB of HBM per device.

v0:
```python
import math

import jax
import jax.numpy as jnp
from jax import lax
from jax.sharding import PartitionSpec as P

FGROUPS = 8
DS = 16


HIGHEST_PRECISION = lax.Precision.HIGHEST


def orthonormal(basis_rows, rank_used):
    ranks = basis_rows.shape[1]
    active = (jnp.arange(ranks) < rank_used).astype(basis_rows.dtype)

    def build_column(column_index, ortho_rows):
        real_part = lax.dynamic_index_in_dim(basis_rows[0], column_index, 0, keepdims=False)
        imag_part = lax.dynamic_index_in_dim(basis_rows[1], column_index, 0, keepdims=False)
        for second in range(2):
            coef_real = jnp.dot(ortho_rows[0], real_part, precision=HIGHEST_PRECISION) + jnp.dot(
                ortho_rows[1], imag_part, precision=HIGHEST_PRECISION
            )
            coef_imag = jnp.dot(ortho_rows[0], imag_part, precision=HIGHEST_PRECISION) - jnp.dot(
                ortho_rows[1], real_part, precision=HIGHEST_PRECISION
            )
            real_part = real_part - (
                jnp.dot(coef_real, ortho_rows[0], precision=HIGHEST_PRECISION)
                - jnp.dot(coef_imag, ortho_rows[1], precision=HIGHEST_PRECISION)
            )
            imag_part = imag_part - (
                jnp.dot(coef_real, ortho_rows[1], precision=HIGHEST_PRECISION)
                + jnp.dot(coef_imag, ortho_rows[0], precision=HIGHEST_PRECISION)
            )
        flag = lax.dynamic_index_in_dim(active, column_index, 0, keepdims=False)
        normalize = flag / jnp.sqrt(
            jnp.sum(real_part * real_part + imag_part * imag_part) + (1.0 - flag)
        )
        new_column = jnp.stack([real_part * normalize, imag_part * normalize])[:, None, :]
        return lax.dynamic_update_slice_in_dim(ortho_rows, new_column, column_index, 1)

    return lax.fori_loop(0, ranks, build_column, jnp.zeros_like(basis_rows))


def half_dot(left, right):
    return jnp.dot(left, right, preferred_element_type=jnp.float32)


def steer_block(row_start, row_count, positions, directions, ortho_rows, frequency):
    chosen = lax.dynamic_slice_in_dim(directions, row_start, row_count, 0)
    phase_angle = (
        2.0
        * jnp.pi
        * frequency
        * (chosen[:, 0:1] * positions[:, 0][None, :] + chosen[:, 1:2] * positions[:, 1][None, :])
    )
    inverse = 1.0 / math.sqrt(positions.shape[0])
    steer_real = jnp.cos(phase_angle) * inverse
    steer_imag = -jnp.sin(phase_angle) * inverse
    short_real = steer_real.astype(jnp.bfloat16)
    short_imag = steer_imag.astype(jnp.bfloat16)
    ortho_real = ortho_rows[0].astype(jnp.bfloat16)
    ortho_imag = ortho_rows[1].astype(jnp.bfloat16)
    along_real = (half_dot(short_real, ortho_real.T) - half_dot(short_imag, ortho_imag.T)).astype(
        jnp.bfloat16
    )
    along_imag = (half_dot(short_real, ortho_imag.T) + half_dot(short_imag, ortho_real.T)).astype(
        jnp.bfloat16
    )
    kept_real = steer_real - (half_dot(along_real, ortho_real) + half_dot(along_imag, ortho_imag))
    kept_imag = steer_imag - (half_dot(along_imag, ortho_real) - half_dot(along_real, ortho_imag))
    return (kept_real.astype(jnp.bfloat16), kept_imag.astype(jnp.bfloat16))


def projected_weights(positions, directions, ortho_rows, frequency):
    beam_count = directions.shape[0]
    row_count = min(beam_count, 512)
    block_count = beam_count // row_count

    def one_block(block_index):
        return steer_block(
            block_index * row_count, row_count, positions, directions, ortho_rows, frequency
        )

    weight_real, weight_imag = lax.map(one_block, jnp.arange(block_count, dtype=jnp.int32))
    input_count = positions.shape[0]
    return (
        weight_real.reshape(beam_count, input_count),
        weight_imag.reshape(beam_count, input_count),
    )


def detect(weight_real, weight_imag, volt_real, volt_imag):
    stacked = jnp.concatenate([volt_real, volt_imag], axis=1)
    frame_count = volt_real.shape[1]
    from_real = jnp.dot(weight_real, stacked, preferred_element_type=jnp.float32)
    from_imag = jnp.dot(weight_imag, stacked, preferred_element_type=jnp.float32)
    beam_real = from_real[:, :frame_count] - from_imag[:, frame_count:]
    beam_imag = from_real[:, frame_count:] + from_imag[:, :frame_count]
    return beam_real * beam_real + beam_imag * beam_imag


def shards(voltages, positions, directions, basis, rank_count):
    inp_size = lax.axis_size("inp")
    chan_size = lax.axis_size("chan")
    per_chan = inp_size // FGROUPS
    channels = chan_size * per_chan
    local_inputs = voltages.shape[2]
    frames_dev = voltages.shape[3] // FGROUPS
    input_count = positions.shape[0]
    beam_count = directions.shape[0]
    sub_channel = lax.axis_index("inp") // FGROUPS
    channel = lax.axis_index("chan") * per_chan + sub_channel
    frequency = 1.0 + 0.5 * channel.astype(jnp.float32) / channels
    rank_used = jnp.sum(jnp.where(jnp.arange(per_chan) == sub_channel, rank_count, 0))
    group_basis = lax.all_gather(basis, "inp", axis=3, tiled=True)
    own_basis = lax.dynamic_index_in_dim(group_basis, sub_channel, 1, keepdims=False)
    sectioned = voltages.reshape(2, chan_size, per_chan, local_inputs, FGROUPS, frames_dev)
    sectioned = jnp.transpose(sectioned, (0, 1, 2, 4, 3, 5)).reshape(
        2, chan_size, inp_size, local_inputs, frames_dev
    )
    ordered_positions = jnp.transpose(
        positions.reshape(inp_size, chan_size, local_inputs, 2), (1, 0, 2, 3)
    ).reshape(input_count, 2)
    ordered_basis = own_basis.reshape(2, own_basis.shape[1], inp_size, chan_size, local_inputs)
    ordered_basis = jnp.transpose(ordered_basis, (0, 1, 3, 2, 4)).reshape(
        2, own_basis.shape[1], input_count
    )
    ortho_rows = orthonormal(ordered_basis, rank_used)
    weight_real, weight_imag = projected_weights(
        ordered_positions, directions, ortho_rows, frequency
    )
    turned = lax.all_to_all(
        lax.all_to_all(sectioned, "inp", split_axis=2, concat_axis=3, tiled=True),
        "chan",
        split_axis=1,
        concat_axis=3,
        tiled=True,
    )
    detected = detect(weight_real, weight_imag, turned[0, 0, 0], turned[1, 0, 0])
    binned = jnp.mean(detected.reshape(beam_count, frames_dev // DS, DS), axis=2)
    regrouped = lax.all_to_all(binned[:, None, :], "inp", split_axis=0, concat_axis=1, tiled=True)
    return regrouped.reshape(beam_count // inp_size, per_chan, FGROUPS * (frames_dev // DS))


def solution(mesh):
    placed = (
        P(None, None, ("inp", "chan"), None),
        P(),
        P(),
        P(None, "chan", None, "inp"),
        P("chan"),
    )
    return jax.shard_map(
        shards, mesh=mesh, in_specs=placed, out_specs=P("inp", "chan", None), check_vma=False
    )
```

profile of v0, /device:TPU:0, one launch (start us, length us, event | category | flops | bytes accessed | tf_op | source)
XLA Modules:
  0.0 308.5 jit_solution(6745723134134475028)
XLA Ops:
  0.0 1.5 copy.50
  1.8 1.1 copy.40
  2.9 7.4 %all-to-all-start = ((bf16[2,2,16,32,256]{4,3,1,0,2:T(8,128)(2,1)}), bf16[2,2,16,32,256]{4,3,1,0,2:T(8,128)(2,1)}, u32[]{:S(2)}, u32[]{:S(2)}) async-start(bf16[2,2,16,32,256]{4,3,1,0,2:T(8,128)(2,1)} %copy.40), calls=%async_computation | async-start | bytes 2097152 | tf_op jit(solution)/shard_map/all_to_all | solution.py:136
  10.5 44.0 %all_gather.3 = f32[2,2,16,1024]{2,1,0,3:T(2,128)S(1)} all-gather(f32[2,2,16,64]{2,1,0,3:T(2,128)S(1)} %copy.36), channel_id=1, replica_groups=mesh['inp'=16,'chan'=2] {'inp'}, dimensions={3}, use_global_device_ids=true | all-gather | bytes 278528 | tf_op jit(solution)/shard_map/all_gather | solution.py:118
  54.4 0.9 constant_dynamic-slice_fusion.3
  57.5 99.3 %while.27 = (s32[]{:T(128)}, f32[2,16,1024]{2,1,0:T(8,128)S(1)}, f32[2,16,1024]{2,1,0:T(8,128)S(1)}, f32[16]{0:T(128)S(1)}, s32[]{:T(128)}, /*index=5*/f32[]{:T(128)}, s32[]{:T(128)}) while((s32[]{:T(128)}, f32[2,16,1024]{2,1,0:T(8,128)S(1)}, f32[2,16,1024]{2,1,0:T(8,128)S(1)}, f32[16]{0:T(128)S(1)}, s32[]{:T(128)}, /*index=5*/f32[]{:T(128)}, ...), condition=%wide.region_3.4_spmd, body=%wide.region_1.3_spmd.sunk | while | flops 3166276 | bytes 1538713 | solution.py:44
  157.0 1.3 copy.41
  158.4 1.1 copy.42
  159.4 3.6 %all-to-all-start.1 = ((bf16[2,2,1,512,256]{4,3,0,2,1:T(8,128)(2,1)}), bf16[2,2,1,512,256]{4,3,0,2,1:T(8,128)(2,1)S(1)}, u32[]{:S(2)}, u32[]{:S(2)}) async-start(bf16[2,2,1,512,256]{4,3,0,2,1:T(8,128)(2,1)} %copy.42), calls=%async_computation.1 | async-start | bytes 2097152 | tf_op jit(solution)/shard_map/all_to_all | solution.py:135
  163.0 122.9 %while.28 = (s32[]{:T(128)}, bf16[2,512,1024]{2,1,0:T(8,128)(2,1)S(1)}, bf16[2,512,1024]{2,1,0:T(8,128)(2,1)}, f32[]{:T(128)}, s32[2]{0:T(128)S(1)}, /*index=5*/...) while((s32[]{:T(128)}, ...), condition=%wide.region_5.6_spmd, body=%wide.region_4.5_spmd.sunk | while | flops 156794880 | bytes 27853100 | solution.py:87
  186.0 0.6 dynamic_slice.43
  187.5 7.2 %fusion.244 = f32[512,16]{0,1:T(8,128)S(1)} fusion(bf16[16,1024]{1,0:T(8,128)(2,1)S(1)} %get-tuple-element.380, f32[1024]{0:T(1024)S(1)} %bitcast.382, f32[512]{0:T(512)S(1)} %bitcast.394, f32[1024]{0:T(1024)S(1)} %bitcast.376, f32[512]{0:T(512)S(1)} %bitcast.388, f32[]{:T(128)} %get-tuple-element.375), kind=kOutput, calls=%fused_computation.85.clone.1 | convolution fusion | flops 19922944 | bytes 77828 | tf_op jit(solution)/shard_map/while/body/eval_jaxpr/dot_general | solution.py:48
  194.7 7.3 %fusion.245 = bf16[512,16]{0,1:T(8,128)(2,1)S(1)} fusion(f32[512,16]{0,1:T(8,128)S(1)} %fusion.244, bf16[16,1024]{1,0:T(8,128)(2,1)S(1)} %get-tuple-element.379, f32[1024]{0:T(1024)S(1)} %bitcast.383, f32[512]{0:T(512)S(1)} %bitcast.395, f32[1024]{0:T(1024)S(1)} %bitcast.377, f32[512]{0:T(512)S(1)} %bitcast.389, f32[]{:T(128)} %get-tuple-element.375), kind=kOutput, calls=%fused_computation.84.clone.1 | convolution fusion | flops 20463616 | bytes 94212 | tf_op jit(solution)/shard_map/while/body/eval_jaxpr/dot_general | solution.py:48
  202.5 7.2 %fusion.241 = f32[512,16]{0,1:T(8,128)S(1)} fusion(bf16[16,1024]{1,0:T(8,128)(2,1)S(1)} %get-tuple-element.379, f32[1024]{0:T(1024)S(1)} %bitcast.384, f32[512]{0:T(512)S(1)} %bitcast.396, f32[1024]{0:T(1024)S(1)} %bitcast.378, f32[512]{0:T(512)S(1)} %bitcast.390, f32[]{:T(128)} %get-tuple-element.375), kind=kOutput, calls=%fused_computation.86.clone.1 | convolution fusion | flops 19922944 | bytes 77828 | tf_op jit(solution)/shard_map/while/body/eval_jaxpr/dot_general | solution.py:48
  209.7 7.3 %fusion.242 = bf16[512,16]{0,1:T(8,128)(2,1)S(1)} fusion(f32[512,16]{0,1:T(8,128)S(1)} %fusion.241, bf16[16,1024]{1,0:T(8,128)(2,1)S(1)} %get-tuple-element.380, f32[1024]{0:T(1024)S(1)} %bitcast.385, f32[512]{0:T(512)S(1)} %bitcast.397, f32[1024]{0:T(1024)S(1)} %bitcast.379, f32[512]{0:T(512)S(1)} %bitcast.391, f32[]{:T(128)} %get-tuple-element.375), kind=kOutput, calls=%fused_computation.83.clone.1 | convolution fusion | flops 20463616 | bytes 94212 | tf_op jit(solution)/shard_map/while/body/eval_jaxpr/dot_general | solution.py:48
  217.0 7.9 %fusion.248 = bf16[2,512,1024]{2,1,0:T(8,128)(2,1)S(1)} fusion(bf16[2,512,1024]{2,1,0:T(8,128)(2,1)S(1)} %copy-done.4, s32[]{:T(128)} %get-tuple-element.358, f32[512,1024]{1,0:T(8,128)S(1)} %fusion.247, bf16[512,16]{0,1:T(8,128)(2,1)S(1)} %fusion.242, bf16[16,1024]{1,0:T(8,128)(2,1)S(1)} %get-tuple-element.380, f32[1024]{0:T(1024)S(1)} %bitcast.386, ...), kind=kOutput, calls=%fused_computation.80.clone.1 | convolution fusion | flops 21495808 | bytes 3207176 | tf_op jit(solution)/shard_map/while/body/eval_jaxpr/dot_general | solution.py:48
  225.3 0.9 copy-done.5
  226.2 7.8 %fusion.246 = bf16[2,512,1024]{2,1,0:T(8,128)(2,1)S(1)} fusion(bf16[2,512,1024]{2,1,0:T(8,128)(2,1)S(1)} %get-tuple-element.359, s32[]{:T(128)} %get-tuple-element.358, f32[512,1024]{1,0:T(8,128)S(1)} %fusion.243, bf16[512,16]{0,1:T(8,128)(2,1)S(1)} %fusion.245, bf16[16,1024]{1,0:T(8,128)(2,1)S(1)} %get-tuple-element.380, f32[1024]{0:T(1024)S(1)} %bitcast.387, ...), kind=kOutput, calls=%fused_computation.78.clone.1 | convolution fusion | flops 20971520 | bytes 3207176 | tf_op jit(solution)/shard_map/while/body/eval_jaxpr/dot_general | solution.py:48
  235.4 7.2 %fusion.244 = f32[512,16]{0,1:T(8,128)S(1)} fusion(bf16[16,1024]{1,0:T(8,128)(2,1)S(1)} %get-tuple-element.380, f32[1024]{0:T(1024)S(1)} %bitcast.382, f32[512]{0:T(512)S(1)} %bitcast.394, f32[1024]{0:T(1024)S(1)} %bitcast.376, f32[512]{0:T(512)S(1)} %bitcast.388, f32[]{:T(128)} %get-tuple-element.375), kind=kOutput, calls=%fused_computation.85.clone.1 | convolution fusion | flops 19922944 | bytes 77828 | tf_op jit(solution)/shard_map/while/body/eval_jaxpr/dot_general | solution.py:48
  242.6 7.3 %fusion.245 = bf16[512,16]{0,1:T(8,128)(2,1)S(1)} fusion(f32[512,16]{0,1:T(8,128)S(1)} %fusion.244, bf16[16,1024]{1,0:T(8,128)(2,1)S(1)} %get-tuple-element.379, f32[1024]{0:T(1024)S(1)} %bitcast.383, f32[512]{0:T(512)S(1)} %bitcast.395, f32[1024]{0:T(1024)S(1)} %bitcast.377, f32[512]{0:T(512)S(1)} %bitcast.389, f32[]{:T(128)} %get-tuple-element.375), kind=kOutput, calls=%fused_computation.84.clone.1 | convolution fusion | flops 20463616 | bytes 94212 | tf_op jit(solution)/shard_map/while/body/eval_jaxpr/dot_general | solution.py:48
  250.4 7.2 %fusion.241 = f32[512,16]{0,1:T(8,128)S(1)} fusion(bf16[16,1024]{1,0:T(8,128)(2,1)S(1)} %get-tuple-element.379, f32[1024]{0:T(1024)S(1)} %bitcast.384, f32[512]{0:T(512)S(1)} %bitcast.396, f32[1024]{0:T(1024)S(1)} %bitcast.378, f32[512]{0:T(512)S(1)} %bitcast.390, f32[]{:T(128)} %get-tuple-element.375), kind=kOutput, calls=%fused_computation.86.clone.1 | convolution fusion | flops 19922944 | bytes 77828 | tf_op jit(solution)/shard_map/while/body/eval_jaxpr/dot_general | solution.py:48
  257.6 7.3 %fusion.242 = bf16[512,16]{0,1:T(8,128)(2,1)S(1)} fusion(f32[512,16]{0,1:T(8,128)S(1)} %fusion.241, bf16[16,1024]{1,0:T(8,128)(2,1)S(1)} %get-tuple-element.380, f32[1024]{0:T(1024)S(1)} %bitcast.385, f32[512]{0:T(512)S(1)} %bitcast.397, f32[1024]{0:T(1024)S(1)} %bitcast.379, f32[512]{0:T(512)S(1)} %bitcast.391, f32[]{:T(128)} %get-tuple-element.375), kind=kOutput, calls=%fused_computation.83.clone.1 | convolution fusion | flops 20463616 | bytes 94212 | tf_op jit(solution)/shard_map/while/body/eval_jaxpr/dot_general | solution.py:48
  264.9 7.9 %fusion.248 = bf16[2,512,1024]{2,1,0:T(8,128)(2,1)S(1)} fusion(bf16[2,512,1024]{2,1,0:T(8,128)(2,1)S(1)} %copy-done.4, s32[]{:T(128)} %get-tuple-element.358, f32[512,1024]{1,0:T(8,128)S(1)} %fusion.247, bf16[512,16]{0,1:T(8,128)(2,1)S(1)} %fusion.242, bf16[16,1024]{1,0:T(8,128)(2,1)S(1)} %get-tuple-element.380, f32[1024]{0:T(1024)S(1)} %bitcast.386, ...), kind=kOutput, calls=%fused_computation.80.clone.1 | convolution fusion | flops 21495808 | bytes 3207176 | tf_op jit(solution)/shard_map/while/body/eval_jaxpr/dot_general | solution.py:48
  273.2 0.9 copy-done.5
  274.1 7.8 %fusion.246 = bf16[2,512,1024]{2,1,0:T(8,128)(2,1)S(1)} fusion(bf16[2,512,1024]{2,1,0:T(8,128)(2,1)S(1)} %get-tuple-element.359, s32[]{:T(128)} %get-tuple-element.358, f32[512,1024]{1,0:T(8,128)S(1)} %fusion.243, bf16[512,16]{0,1:T(8,128)(2,1)S(1)} %fusion.245, bf16[16,1024]{1,0:T(8,128)(2,1)S(1)} %get-tuple-element.380, f32[1024]{0:T(1024)S(1)} %bitcast.387, ...), kind=kOutput, calls=%fused_computation.78.clone.1 | convolution fusion | flops 20971520 | bytes 3207176 | tf_op jit(solution)/shard_map/while/body/eval_jaxpr/dot_general | solution.py:48
  286.0 1.3 fusion.74
  287.6 1.3 fusion.73
  290.0 0.7 reduce
  291.1 14.4 %all_to_all.36 = f32[16,1,1024]{2,1,0:T(1,128)S(1)} all-to-all(f32[16,1,1024]{2,1,0:T(1,128)S(1)} %reshape.105), channel_id=1, replica_groups=mesh['inp'=16,'chan'=2] {'inp'}, dimensions={0} | all-to-all | bytes 131072 | tf_op jit(solution)/shard_map/all_to_all | solution.py:144
  305.6 0.8 reduce.1
  306.4 0.9 reshape.106
  307.6 0.7 copy.46
  (482 shorter events, 74.7 us)
Async XLA Ops:
  1.8 8.5 %copy-start.1 = (f32[2,2,16,64]{3,2,1,0:T(8,128)S(1)}, f32[2,2,16,64]{3,2,1,0:T(8,128)}, u32[]{:S(2)}) copy-start(f32[2,2,16,64]{3,2,1,0:T(8,128)} %param.12) | copy-start | bytes 49156
  2.9 154.2 %all-to-all-start = ((bf16[2,2,16,32,256]{4,3,1,0,2:T(8,128)(2,1)}), bf16[2,2,16,32,256]{4,3,1,0,2:T(8,128)(2,1)}, u32[]{:S(2)}, u32[]{:S(2)}) async-start(bf16[2,2,16,32,256]{4,3,1,0,2:T(8,128)(2,1)} %copy.40), calls=%async_computation | async-start | bytes 2097152 | tf_op jit(solution)/shard_map/all_to_all | solution.py:136
  54.4 1.7 copy-start.3
  57.4 99.4 %copy-start.2 = (f32[1024,2]{0,1:T(2,128)S(1)}, f32[1024,2]{0,1:T(2,128)}, u32[]{:S(2)}) copy-start(f32[1024,2]{0,1:T(2,128)} %param.10) | copy-start | bytes 24580
  158.3 4.7 %copy-start = (f32[1024,2]{0,1:T(2,128)S(1)}, f32[1024,2]{0,1:T(2,128)}, u32[]{:S(2)}) copy-start(f32[1024,2]{0,1:T(2,128)} %param.11) | copy-start | bytes 24580
  159.4 126.5 %all-to-all-start.1 = ((bf16[2,2,1,512,256]{4,3,0,2,1:T(8,128)(2,1)}), bf16[2,2,1,512,256]{4,3,0,2,1:T(8,128)(2,1)S(1)}, u32[]{:S(2)}, u32[]{:S(2)}) async-start(bf16[2,2,1,512,256]{4,3,0,2,1:T(8,128)(2,1)} %copy.42), calls=%async_computation.1 | async-start | bytes 2097152 | tf_op jit(solution)/shard_map/all_to_all | solution.py:135
  209.7 7.3 %copy-start.4 = (bf16[2,512,1024]{2,1,0:T(8,128)(2,1)S(1)}, bf16[2,512,1024]{2,1,0:T(8,128)(2,1)}, u32[]{:S(2)}) copy-start(bf16[2,512,1024]{2,1,0:T(8,128)(2,1)} %get-tuple-element.360) | copy-start | bytes 6291460 | tf_op jit(solution)/shard_map/while
  224.9 1.3 copy-start.5
  257.6 7.3 %copy-start.4 = (bf16[2,512,1024]{2,1,0:T(8,128)(2,1)S(1)}, bf16[2,512,1024]{2,1,0:T(8,128)(2,1)}, u32[]{:S(2)}) copy-start(bf16[2,512,1024]{2,1,0:T(8,128)(2,1)} %get-tuple-element.360) | copy-start | bytes 6291460 | tf_op jit(solution)/shard_map/while
  272.8 1.3 copy-start.5
  286.0 1.6 copy-start.6
where the time goes:
time: 313 us; the launch traced here: 308 us
  matrix products  139 us (44%)
  loops' own time  60.6 us (19%)
  blocking collectives  58.4 us (19%)
  local copies, waits for them, and re-layouts  25.5 us (8%)
  other arithmetic  13.5 us (4%)
  starting transfers between devices  11 us (4%)
    dot_general x16, matrix products, half_dot(): return jnp.dot(left, right, preferred_element_type=jnp.float32)  91.2 us
    all_gather x1, blocking collectives, shards(): group_basis = lax.all_gather(basis, 'inp', axis=3, tiled=True)  44 us
    another operation x1, loops' own time, orthonormal(): return lax.fori_loop(0, ranks, build_column, jnp.zeros_like(basis_rows))  32 us
    another operation x1, loops' own time, projected_weights(): lax.map(one_block, jnp.arange(block_count, dtype=jnp.int32))  28.5 us
    all_to_all x1, blocking collectives, shards(): lax.all_to_all(binned[:, None, :], 'inp', split_axis=0, concat_axis=1, ti...  14.4 us
    reduce_sum x16, other arithmetic, build_column(): jnp.sum(real_part * real_part + imag_part * imag_part) + (1.0 - flag)  9.59 us
    dynamic_slice x16, local copies, waits for them, and re-layouts, build_column(): flag = lax.dynamic_index_in_dim(active, column_index, 0, keepdims=False)  9.46 us
    all_to_all x1, starting transfers between devices, shards(): lax.all_to_all(sectioned, 'inp', split_axis=2, concat_axis=3, tiled=True)  7.41 us
  transfers between devices with their start and end apart: 2, of which 0 were waited for; matrix products, arithmetic and copies ran while one was open for 53% of the time, Pallas kernels for 0%

commit v1 on v0

--- a/solution.py
+++ b/solution.py
@@ -1,12 +1,18 @@
+import functools
 import math
 
 import jax
 import jax.numpy as jnp
+import numpy as np
 from jax import lax
+from jax.experimental import pallas as pl
+from jax.experimental.pallas import tpu as pltpu
 from jax.sharding import PartitionSpec as P
 
 FGROUPS = 8
 DS = 16
+ROWS = 128
+MESH = pl.DeviceIdType.MESH
 
 
 HIGHEST_PRECISION = lax.Precision.HIGHEST
@@ -145,6 +151,364 @@
     return regrouped.reshape(beam_count // inp_size, per_chan, FGROUPS * (frames_dev // DS))
 
 
+def turn_coefficients(input_count):
+    nodes = np.cos(np.pi * (np.arange(400) + 0.5) / 400) * 0.25 * 0.5 + 0.125
+    root = np.sqrt(nodes)
+    scale = 1.0 / math.sqrt(input_count)
+    fit = np.polynomial.chebyshev.Chebyshev.fit
+    power = np.polynomial.Polynomial
+    sin_fit = fit(nodes, np.sin(2 * np.pi * root) / root, 6, domain=[0, 0.25]).convert(kind=power)
+    cos_fit = fit(nodes, np.cos(2 * np.pi * root), 7, domain=[0, 0.25]).convert(kind=power)
+    return (
+        [float(value) * scale for value in sin_fit.coef],
+        [float(value) * scale for value in cos_fit.coef],
+    )
+
+
+def horner(coefs, x):
+    total = jnp.full_like(x, coefs[-1])
+    for value in coefs[-2::-1]:
+        total = total * x + value
+    return total
+
+
+def across(left, right):
+    return lax.dot_general(
+        left, right, (((1,), (1,)), ((), ())), preferred_element_type=jnp.float32
+    )
+
+
+def fused_kernel(
+    sizes,
+    volt_ref,
+    pos_ref,
+    dir_ref,
+    basis_ref,
+    rank_ref,
+    out_ref,
+    turned,
+    basis_in,
+    rows_real,
+    rows_imag,
+    ortho_real,
+    ortho_imag,
+    ortho_half,
+    weight_real,
+    weight_imag,
+    power_out,
+    power_in,
+    local_sem,
+    volt_send,
+    volt_recv,
+    basis_send,
+    basis_recv,
+    power_send,
+    power_recv,
+):
+    inp_size, chan_size, per_chan, beam_count, frames_dev = sizes
+    devices = inp_size * chan_size
+    local_inputs = volt_ref.shape[2]
+    input_count = pos_ref.shape[1]
+    ranks = basis_ref.shape[2]
+    my_inp = lax.axis_index("inp")
+    my_chan = lax.axis_index("chan")
+    me = my_inp * chan_size + my_chan
+    sub = my_inp // FGROUPS
+    samples = frames_dev // DS
+    beams_each = beam_count // inp_size
+    owners = ROWS // beams_each
+    blocks = beam_count // ROWS
+
+    def device(number):
+        return (number // chan_size, lax.rem(number, chan_size))
+
+    def other(k):
+        return lax.rem(me + k, devices)
+
+    def other_inp(k):
+        return lax.rem(my_inp + k, inp_size)
+
+    barrier = pltpu.get_barrier_semaphore()
+
+    def greet(k, carry):
+        pl.semaphore_signal(barrier, inc=1, device_id=device(other(k)), device_id_type=MESH)
+        return carry
+
+    lax.fori_loop(1, devices, greet, 0)
+    pl.semaphore_wait(barrier, devices - 1)
+
+    def basis_copy(target, slot):
+        return pltpu.make_async_remote_copy(
+            src_ref=basis_ref.at[:, target // FGROUPS],
+            dst_ref=basis_in.at[slot],
+            send_sem=basis_send.at[target],
+            recv_sem=basis_recv.at[slot],
+            device_id=(target, my_chan),
+            device_id_type=MESH,
+        )
+
+    def volt_block(target):
+        target_inp = target // chan_size
+        channel = lax.rem(target, chan_size) * per_chan + target_inp // FGROUPS
+        start = pl.multiple_of(lax.rem(target_inp, FGROUPS) * frames_dev, frames_dev)
+        return volt_ref.at[:, channel, :, pl.ds(start, frames_dev)]
+
+    def turned_block(slot):
+        return turned.at[
+            :, pl.ds(pl.multiple_of(slot * local_inputs, local_inputs), local_inputs), :
+        ]
+
+    def volt_copy(target, slot):
+        return pltpu.make_async_remote_copy(
+            src_ref=volt_block(target),
+            dst_ref=turned_block(slot),
+            send_sem=volt_send.at[target],
+            recv_sem=volt_recv.at[slot],
+            device_id=device(target),
+            device_id_type=MESH,
+        )
+
+    def power_copy(target, slot):
+        return pltpu.make_async_remote_copy(
+            src_ref=power_out.at[target],
+            dst_ref=power_in.at[slot],
+            send_sem=power_send.at[target],
+            recv_sem=power_recv.at[slot],
+            device_id=(target, my_chan),
+            device_id_type=MESH,
+        )
+
+    def send_basis(k, carry):
+        basis_copy(other_inp(k), my_inp).start()
+        return carry
+
+    lax.fori_loop(1, inp_size, send_basis, 0)
+
+    def send_volt(k, carry):
+        volt_copy(other(k), me).start()
+        return carry
+
+    lax.fori_loop(1, devices, send_volt, 0)
+    own = pltpu.make_async_copy(volt_block(me), turned_block(me), local_sem)
+    own.start()
+
+    basis_in[my_inp] = basis_ref[:, sub]
+
+    def take_basis(k, carry):
+        basis_copy(other_inp(k), other_inp(k)).wait_recv()
+        return carry
+
+    lax.fori_loop(1, inp_size, take_basis, 0)
+    rows_real[...] = jnp.concatenate([basis_in[s, 0] for s in range(inp_size)], axis=1)
+    rows_imag[...] = jnp.concatenate([basis_in[s, 1] for s in range(inp_size)], axis=1)
+    ortho_real[...] = jnp.zeros_like(ortho_real)
+    ortho_imag[...] = jnp.zeros_like(ortho_imag)
+    rank_used = rank_ref[sub]
+
+    def build_row(row, carry):
+        real_part = rows_real[pl.ds(row, 1), :]
+        imag_part = rows_imag[pl.ds(row, 1), :]
+        for second in range(2):
+            real_rows, imag_rows = ortho_real[...], ortho_imag[...]
+            coef_real = jnp.sum(
+                real_rows * real_part + imag_rows * imag_part, axis=1, keepdims=True
+            )
+            coef_imag = jnp.sum(
+                real_rows * imag_part - imag_rows * real_part, axis=1, keepdims=True
+            )
+            real_part = real_part - jnp.sum(
+                coef_real * real_rows - coef_imag * imag_rows, axis=0, keepdims=True
+            )
+            imag_part = imag_part - jnp.sum(
+                coef_real * imag_rows + coef_imag * real_rows, axis=0, keepdims=True
+            )
+        flag = jnp.where(row < rank_used, 1.0, 0.0).astype(jnp.float32)
+        square = jnp.sum(
+            real_part * real_part + imag_part * imag_part, axis=1, keepdims=True
+        )
+        normalize = flag / jnp.sqrt(square + (1.0 - flag))
+        ortho_real[pl.ds(row, 1), :] = real_part * normalize
+        ortho_imag[pl.ds(row, 1), :] = imag_part * normalize
+        return carry
+
+    lax.fori_loop(0, ranks, build_row, 0)
+    ortho_half[...] = jnp.concatenate([ortho_real[...], ortho_imag[...]], axis=0).astype(
+        jnp.bfloat16
+    )
+
+    channel = my_chan * per_chan + sub
+    frequency = 1.0 + 0.5 * channel.astype(jnp.float32) / (chan_size * per_chan)
+    sin_coefs, cos_coefs = turn_coefficients(input_count)
+
+    def weigh(block, carry):
+        rows = pl.ds(pl.multiple_of(block * ROWS, ROWS), ROWS)
+        first = jnp.broadcast_to(dir_ref[0:1, rows], (ROWS, ROWS)).T
+        second = jnp.broadcast_to(dir_ref[1:2, rows], (ROWS, ROWS)).T
+        reals, imags = [], []
+        for piece in range(input_count // ROWS):
+            lanes = slice(piece * ROWS, (piece + 1) * ROWS)
+            turns = first * (pos_ref[0:1, lanes] * frequency) + second * (
+                pos_ref[1:2, lanes] * frequency
+            )
+            turns = turns - jnp.round(turns)
+            square = turns * turns
+            reals.append(horner(cos_coefs, square))
+            imags.append(-turns * horner(sin_coefs, square))
+        steer_real = jnp.concatenate(reals, axis=1)
+        steer_imag = jnp.concatenate(imags, axis=1)
+        half = ortho_half[...]
+        from_real = across(steer_real.astype(jnp.bfloat16), half)
+        from_imag = across(steer_imag.astype(jnp.bfloat16), half)
+        along_real = from_real[:, :ranks] - from_imag[:, ranks:]
+        along_imag = from_real[:, ranks:] + from_imag[:, :ranks]
+        for_real = jnp.concatenate([along_real, along_imag], axis=1).astype(jnp.bfloat16)
+        for_imag = jnp.concatenate([along_imag, -along_real], axis=1).astype(jnp.bfloat16)
+        weight_real[rows, :] = (steer_real - half_dot(for_real, half)).astype(jnp.bfloat16)
+        weight_imag[rows, :] = (steer_imag - half_dot(for_imag, half)).astype(jnp.bfloat16)
+        return carry
+
+    lax.fori_loop(0, blocks, weigh, 0)
+
+    def take_volt(k, carry):
+        volt_copy(other(k), other(k)).wait_recv()
+        return carry
+
+    own.wait()
+    lax.fori_loop(1, devices, take_volt, 0)
+
+    sample_row = lax.broadcasted_iota(jnp.int32, (samples, frames_dev), 0)
+    frame_column = lax.broadcasted_iota(jnp.int32, (samples, frames_dev), 1)
+    inside = (frame_column >= sample_row * DS) & (frame_column < sample_row * DS + DS)
+    pool = jnp.where(inside, 1.0 / DS, 0.0).astype(jnp.bfloat16)
+
+    def form(step, carry):
+        block = lax.rem(step + my_inp // owners, blocks)
+        rows = pl.ds(pl.multiple_of(block * ROWS, ROWS), ROWS)
+        volt_real, volt_imag = turned[0], turned[1]
+        left, right = weight_real[rows, :], weight_imag[rows, :]
+        beam_real = half_dot(left, volt_real) - half_dot(right, volt_imag)
+        beam_imag = half_dot(left, volt_imag) + half_dot(right, volt_real)
+        power = beam_real * beam_real + beam_imag * beam_imag
+        high = power.astype(jnp.bfloat16)
+        rest = power - high.astype(jnp.float32)
+        middle = rest.astype(jnp.bfloat16)
+        low = (rest - middle.astype(jnp.float32)).astype(jnp.bfloat16)
+        binned = across(pool, high) + across(pool, middle) + across(pool, low)
+        for part in range(owners):
+            target = block * owners + part
+            piece = binned[:, part * beams_each : (part + 1) * beams_each]
+
+            @pl.when(target == my_inp)
+            def keep():
+                power_in[my_inp] = piece
+
+            @pl.when(target != my_inp)
+            def pass_on():
+                power_out[target] = piece
+                power_copy(target, my_inp).start()
+
+        return carry
+
+    lax.fori_loop(0, blocks, form, 0)
+
+    def take_power(k, carry):
+        power_copy(other_inp(k), other_inp(k)).wait_recv()
+        return carry
+
+    lax.fori_loop(1, inp_size, take_power, 0)
+    for index in range(per_chan):
+        group = [power_in[index * FGROUPS + f] for f in range(FGROUPS)]
+        out_ref[index] = jnp.concatenate(group, axis=0).T
+
+    def finish_inp(k, carry):
+        basis_copy(other_inp(k), my_inp).wait_send()
+        power_copy(other_inp(k), my_inp).wait_send()
+        return carry
+
+    lax.fori_loop(1, inp_size, finish_inp, 0)
+
+    def finish_volt(k, carry):
+        volt_copy(other(k), me).wait_send()
+        return carry
+
+    lax.fori_loop(1, devices, finish_volt, 0)
+
+
+def fused(voltages, positions, directions, basis, rank_count):
+    inp_size = lax.axis_size("inp")
+    chan_size = lax.axis_size("chan")
+    devices = inp_size * chan_size
+    per_chan = inp_size // FGROUPS
+    frames_dev = voltages.shape[3] // FGROUPS
+    input_count = positions.shape[0]
+    beam_count = directions.shape[0]
+    ranks = basis.shape[2]
+    basis_lanes = basis.shape[3]
+    samples = frames_dev // DS
+    beams_each = beam_count // inp_size
+    sizes = (inp_size, chan_size, per_chan, beam_count, frames_dev)
+    vmem = pl.BlockSpec(memory_space=pltpu.VMEM)
+    dma = pltpu.SemaphoreType.DMA
+    row_block = pltpu.VMEM((ranks, input_count), jnp.float32)
+    weight = pltpu.VMEM((beam_count, input_count), jnp.bfloat16)
+    result = pl.pallas_call(
+        functools.partial(fused_kernel, sizes),
+        out_shape=jax.ShapeDtypeStruct(
+            (per_chan, beams_each, FGROUPS * samples), jnp.float32
+        ),
+        in_specs=[
+            pl.BlockSpec(memory_space=pl.ANY),
+            vmem,
+            vmem,
+            vmem,
+            pl.BlockSpec(memory_space=pltpu.SMEM),
+        ],
+        out_specs=vmem,
+        scratch_shapes=[
+            pltpu.VMEM((2, input_count, frames_dev), jnp.bfloat16),
+            pltpu.VMEM((inp_size, 2, ranks, basis_lanes), jnp.float32),
+            row_block,
+            row_block,
+            row_block,
+            row_block,
+            pltpu.VMEM((2 * ranks, input_count), jnp.bfloat16),
+            weight,
+            weight,
+            pltpu.VMEM((inp_size, samples, beams_each), jnp.float32),
+            pltpu.VMEM((inp_size, samples, beams_each), jnp.float32),
+            dma,
+            dma((devices,)),
+            dma((devices,)),
+            dma((inp_size,)),
+            dma((inp_size,)),
+            dma((inp_size,)),
+            dma((inp_size,)),
+        ],
+        compiler_params=pltpu.CompilerParams(
+            collective_id=0, has_side_effects=True, vmem_limit_bytes=40 * 1024 * 1024
+        ),
+    )(voltages, positions.T, directions.T, basis, rank_count)
+    return jnp.transpose(result, (1, 0, 2))
+
+
+def fits(mesh_sizes, voltages, positions, directions):
+    inp_size, chan_size = mesh_sizes
+    beams_each = directions.shape[0] // inp_size
+    return (
+        voltages.shape[2] % 16 == 0
+        and (voltages.shape[3] // FGROUPS) % 128 == 0
+        and positions.shape[0] % ROWS == 0
+        and directions.shape[0] % ROWS == 0
+        and ROWS % beams_each == 0
+    )
+
+
+def either(voltages, positions, directions, basis, rank_count):
+    mesh_sizes = (lax.axis_size("inp"), lax.axis_size("chan"))
+    way = fused if fits(mesh_sizes, voltages, positions, directions) else shards
+    return way(voltages, positions, directions, basis, rank_count)
+
+
 def solution(mesh):
     placed = (
         P(None, None, ("inp", "chan"), None),
@@ -154,5 +518,5 @@
         P("chan"),
     )
     return jax.shard_map(
-        shards, mesh=mesh, in_specs=placed, out_specs=P("inp", "chan", None), check_vma=False
-    )
+        either, mesh=mesh, in_specs=placed, out_specs=P("inp", "chan", None), check_vma=False
+    )

time: 313 us -> 55.7 us (0.18); the launches traced: 308 us -> 55.4 us
  matrix products: 139 us -> 0 us
  loops' own time: 60.6 us -> 0 us
  blocking collectives: 58.4 us -> 0 us
  Pallas kernels: 0 us -> 50.7 us
  local copies, waits for them, and re-layouts: 25.5 us -> 4.71 us
  other arithmetic: 13.5 us -> 0 us
  starting transfers between devices: 11 us -> 0 us
    dot_general x274 -> x0, matrix products: 139 us -> none  [the longest x16 91.2 us: half_dot(): return jnp.dot(left, right, preferred_element_type=jnp.float32)]
    another operation x2 -> x0, loops' own time: 60.6 us -> none  [the longest x1 32 us: orthonormal(): return lax.fori_loop(0, ranks, build_column, jnp.zeros_like(basis_rows))]
    pallas_call x0 -> x1, Pallas kernels: none -> 50.7 us  [fused(): pl.pallas_call(functools.partial(fused_kernel, sizes), out_shape=jax.Shap...]
    all_gather x1 -> x0, blocking collectives: 44 us -> none  [shards(): group_basis = lax.all_gather(basis, 'inp', axis=3, tiled=True)]
    all_to_all x1 -> x0, blocking collectives: 14.4 us -> none  [shards(): lax.all_to_all(binned[:, None, :], 'inp', split_axis=0, concat_axis=1, ti...]
    dynamic_slice x35 -> x0, local copies, waits for them, and re-layouts: 11.9 us -> none  [the longest x16 9.46 us: build_column(): flag = lax.dynamic_index_in_dim(active, column_index, 0, keepdims=False)]
    all_to_all x2 -> x0, starting transfers between devices: 11 us -> none  [the longest x1 7.41 us: shards(): lax.all_to_all(sectioned, 'inp', split_axis=2, concat_axis=3, tiled=True)]
    reduce_sum x18 -> x0, other arithmetic: 10.8 us -> none  [the longest x16 9.59 us: build_column(): jnp.sum(real_part * real_part + imag_part * imag_part) + (1.0 - flag)]
  transfers between devices with their start and end apart: 2 -> 0, of which waited for: 0 -> 0; matrix products, arithmetic and copies ran while one was open for 53% -> 0% of each run, Pallas kernels for 0% -> 0%
where the time goes in v1:
time: 55.7 us; the launch traced here: 55.4 us
  Pallas kernels  50.7 us (91%)
  local copies, waits for them, and re-layouts  4.71 us (8%)
    pallas_call x1, Pallas kernels, fused(): pl.pallas_call(functools.partial(fused_kernel, sizes), out_shape=jax.Shap...  50.7 us
    unnamed x10, local copies, waits for them, and re-layouts  4.03 us

profile of v1, /device:TPU:0, one launch (start us, length us, event | category | flops | bytes accessed | tf_op | source)
XLA Modules:
  0.0 55.4 jit_solution(16481355688854544273)
XLA Ops:
  0.0 0.0 copy-start.4
  0.0 0.7 %copy-done.4 = s32[2]{0:T(128)S(1)} copy-done((s32[2]{0:T(128)S(1)}, s32[2]{0:T(128)}, u32[]{:S(2)}) %copy-start.4) | copy-done | bytes 32
  0.7 0.0 copy-start
  0.7 1.2 %copy-done = bf16[2,4,32,2048]{3,2,1,0:T(8,128)(2,1)S(1)} copy-done((bf16[2,4,32,2048]{3,2,1,0:T(8,128)(2,1)S(1)}, bf16[2,4,32,2048]{3,2,1,0:T(8,128)(2,1)}, u32[]{:S(2)}) %copy-start) | copy-done | bytes 1048600
  1.9 0.0 copy-start.1
  1.9 0.8 %copy-done.1 = f32[2,2,16,64]{3,2,1,0:T(8,128)S(1)} copy-done((f32[2,2,16,64]{3,2,1,0:T(8,128)S(1)}, f32[2,2,16,64]{3,2,1,0:T(8,128)}, u32[]{:S(2)}) %copy-start.1) | copy-done | bytes 16408
  2.6 0.0 copy-start.2
  2.6 0.7 %copy-done.2 = f32[1024,2]{0,1:T(2,128)S(1)} copy-done((f32[1024,2]{0,1:T(2,128)S(1)}, f32[1024,2]{0,1:T(2,128)}, u32[]{:S(2)}) %copy-start.2) | copy-done | bytes 8216
  3.3 0.0 copy-start.3
  3.3 0.7 %copy-done.3 = f32[1024,2]{0,1:T(2,128)S(1)} copy-done((f32[1024,2]{0,1:T(2,128)S(1)}, f32[1024,2]{0,1:T(2,128)}, u32[]{:S(2)}) %copy-start.3) | copy-done | bytes 8216
  4.0 50.7 %shard_map.55 = f32[2,64,128]{2,1,0:T(8,128)S(1)} custom-call(bf16[2,4,32,2048]{3,2,1,0:T(8,128)(2,1)S(1)} %copy-done, f32[2,1024]{1,0:T(2,128)S(1)} %bitcast.4, f32[2,1024]{1,0:T(2,128)S(1)} %bitcast.5, f32[2,2,16,64]{3,2,1,0:T(8,128)S(1)} %copy-done.1, s32[2]{0:T(128)S(1)} %copy-done.4), custom_call_target="tpu_custom_call" | custom-call | tf_op jit(solution)/shard_map/pallas_call | solution.py:454
  54.7 0.7 %copy.6 = f32[64,2,128]{2,1,0:T(2,128)} copy(f32[64,2,128]{2,0,1:T(8,128)S(1)} %bitcast.3) | data formatting | bytes 131072 | tf_op jit(solution)/shard_map/transpose | solution.py:491
Async XLA Ops:
  0.0 0.7 %copy-start.4 = (s32[2]{0:T(128)S(1)}, s32[2]{0:T(128)}, u32[]{:S(2)}) copy-start(s32[2]{0:T(128)} %rank_ref.1) | copy-start | bytes 28
  0.7 1.2 %copy-start = (bf16[2,4,32,2048]{3,2,1,0:T(8,128)(2,1)S(1)}, bf16[2,4,32,2048]{3,2,1,0:T(8,128)(2,1)}, u32[]{:S(2)}) copy-start(bf16[2,4,32,2048]{3,2,1,0:T(8,128)(2,1)} %volt_ref.1) | copy-start | bytes 3145732
  1.9 0.8 %copy-start.1 = (f32[2,2,16,64]{3,2,1,0:T(8,128)S(1)}, f32[2,2,16,64]{3,2,1,0:T(8,128)}, u32[]{:S(2)}) copy-start(f32[2,2,16,64]{3,2,1,0:T(8,128)} %basis_ref.1) | copy-start | bytes 49156
  2.6 0.7 %copy-start.2 = (f32[1024,2]{0,1:T(2,128)S(1)}, f32[1024,2]{0,1:T(2,128)}, u32[]{:S(2)}) copy-start(f32[1024,2]{0,1:T(2,128)} %param.6) | copy-start | bytes 24580
  3.3 0.7 %copy-start.3 = (f32[1024,2]{0,1:T(2,128)S(1)}, f32[1024,2]{0,1:T(2,128)}, u32[]{:S(2)}) copy-start(f32[1024,2]{0,1:T(2,128)} %param.7) | copy-start | bytes 24580

commit v2 on v1

--- a/solution.py
+++ b/solution.py
@@ -12,6 +12,7 @@
 FGROUPS = 8
 DS = 16
 ROWS = 128
+FORM_ROWS = 256
 MESH = pl.DeviceIdType.MESH
 
 
@@ -157,8 +158,8 @@
     scale = 1.0 / math.sqrt(input_count)
     fit = np.polynomial.chebyshev.Chebyshev.fit
     power = np.polynomial.Polynomial
-    sin_fit = fit(nodes, np.sin(2 * np.pi * root) / root, 6, domain=[0, 0.25]).convert(kind=power)
-    cos_fit = fit(nodes, np.cos(2 * np.pi * root), 7, domain=[0, 0.25]).convert(kind=power)
+    sin_fit = fit(nodes, np.sin(2 * np.pi * root) / root, 5, domain=[0, 0.25]).convert(kind=power)
+    cos_fit = fit(nodes, np.cos(2 * np.pi * root), 6, domain=[0, 0.25]).convert(kind=power)
     return (
         [float(value) * scale for value in sin_fit.coef],
         [float(value) * scale for value in cos_fit.coef],
@@ -181,12 +182,17 @@
 def fused_kernel(
     sizes,
     volt_ref,
+    pos_hbm,
+    dir_hbm,
+    basis_hbm,
+    rank_hbm,
+    out_ref,
     pos_ref,
     dir_ref,
     basis_ref,
     rank_ref,
-    out_ref,
     turned,
+    packed,
     basis_in,
     rows_real,
     rows_imag,
@@ -198,6 +204,7 @@
     power_out,
     power_in,
     local_sem,
+    stage_sem,
     volt_send,
     volt_recv,
     basis_send,
@@ -216,8 +223,11 @@
     sub = my_inp // FGROUPS
     samples = frames_dev // DS
     beams_each = beam_count // inp_size
-    owners = ROWS // beams_each
+    owners = FORM_ROWS // beams_each
     blocks = beam_count // ROWS
+    form_blocks = beam_count // FORM_ROWS
+    place = lax.rem(my_inp, FGROUPS)
+    half = devices // per_chan
 
     def device(number):
         return (number // chan_size, lax.rem(number, chan_size))
@@ -228,6 +238,23 @@
     def other_inp(k):
         return lax.rem(my_inp + k, inp_size)
 
+    pairs = (
+        (basis_hbm, basis_ref),
+        (pos_hbm, pos_ref),
+        (dir_hbm, dir_ref),
+        (rank_hbm, rank_ref),
+    )
+    staged = [
+        pltpu.make_async_copy(far, near, stage_sem.at[index])
+        for index, (far, near) in enumerate(pairs)
+    ]
+    for copy in staged:
+        copy.start()
+
+    def spread(k):
+        target_sub = lax.rem(sub + 1 + k // half, per_chan)
+        return target_sub * half + lax.rem(me + k, half)
+
     barrier = pltpu.get_barrier_semaphore()
 
     def greet(k, carry):
@@ -235,17 +262,35 @@
         return carry
 
     lax.fori_loop(1, devices, greet, 0)
+    staged[0].wait()
+    for index in range(per_chan):
+        packed[index] = jnp.concatenate([basis_ref[0, index], basis_ref[1, index]], axis=1)
+    basis_in[my_inp] = packed[sub]
     pl.semaphore_wait(barrier, devices - 1)
 
-    def basis_copy(target, slot):
+    def basis_cross(target_sub, slot):
+        target = target_sub * FGROUPS + place
         return pltpu.make_async_remote_copy(
-            src_ref=basis_ref.at[:, target // FGROUPS],
+            src_ref=packed.at[target_sub],
             dst_ref=basis_in.at[slot],
             send_sem=basis_send.at[target],
             recv_sem=basis_recv.at[slot],
             device_id=(target, my_chan),
             device_id_type=MESH,
         )
+
+    def basis_near(slot, peer):
+        return pltpu.make_async_remote_copy(
+            src_ref=basis_in.at[slot],
+            dst_ref=basis_in.at[slot],
+            send_sem=basis_send.at[slot // FGROUPS * FGROUPS + peer],
+            recv_sem=basis_recv.at[slot],
+            device_id=(sub * FGROUPS + peer, my_chan),
+            device_id_type=MESH,
+        )
+
+    def peer(k):
+        return lax.rem(place + k, FGROUPS)
 
     def volt_block(target):
         target_inp = target // chan_size
@@ -278,29 +323,42 @@
             device_id_type=MESH,
         )
 
-    def send_basis(k, carry):
-        basis_copy(other_inp(k), my_inp).start()
-        return carry
-
-    lax.fori_loop(1, inp_size, send_basis, 0)
+    for offset in range(1, per_chan):
+        basis_cross(lax.rem(sub + offset, per_chan), my_inp).start()
+
+    def pass_basis(slot):
+        def body(k, carry):
+            basis_near(slot, peer(k)).start()
+            return carry
+
+        lax.fori_loop(1, FGROUPS, body, 0)
+
+    pass_basis(my_inp)
 
     def send_volt(k, carry):
-        volt_copy(other(k), me).start()
-        return carry
-
-    lax.fori_loop(1, devices, send_volt, 0)
+        volt_copy(spread(k), me).start()
+        return carry
+
+    lax.fori_loop(0, devices - half, send_volt, 0)
+    for offset in range(1, per_chan):
+        source = lax.rem(sub + offset, per_chan) * FGROUPS + place
+        basis_near(source, place).wait_recv()
+        pass_basis(source)
+    lax.fori_loop(devices - half + 1, devices, send_volt, 0)
     own = pltpu.make_async_copy(volt_block(me), turned_block(me), local_sem)
     own.start()
-
-    basis_in[my_inp] = basis_ref[:, sub]
-
-    def take_basis(k, carry):
-        basis_copy(other_inp(k), other_inp(k)).wait_recv()
-        return carry
-
-    lax.fori_loop(1, inp_size, take_basis, 0)
-    rows_real[...] = jnp.concatenate([basis_in[s, 0] for s in range(inp_size)], axis=1)
-    rows_imag[...] = jnp.concatenate([basis_in[s, 1] for s in range(inp_size)], axis=1)
+    for copy in staged[1:]:
+        copy.wait()
+
+    def take_basis(index, carry):
+        slot = index // (FGROUPS - 1) * FGROUPS + peer(lax.rem(index, FGROUPS - 1) + 1)
+        basis_near(slot, place).wait_recv()
+        return carry
+
+    lax.fori_loop(0, per_chan * (FGROUPS - 1), take_basis, 0)
+    lanes_each = basis_ref.shape[3]
+    rows_real[...] = jnp.concatenate([basis_in[s, :, :lanes_each] for s in range(inp_size)], axis=1)
+    rows_imag[...] = jnp.concatenate([basis_in[s, :, lanes_each:] for s in range(inp_size)], axis=1)
     ortho_real[...] = jnp.zeros_like(ortho_real)
     ortho_imag[...] = jnp.zeros_like(ortho_imag)
     rank_used = rank_ref[sub]
@@ -382,8 +440,8 @@
     pool = jnp.where(inside, 1.0 / DS, 0.0).astype(jnp.bfloat16)
 
     def form(step, carry):
-        block = lax.rem(step + my_inp // owners, blocks)
-        rows = pl.ds(pl.multiple_of(block * ROWS, ROWS), ROWS)
+        block = lax.rem(step + my_inp // owners, form_blocks)
+        rows = pl.ds(pl.multiple_of(block * FORM_ROWS, FORM_ROWS), FORM_ROWS)
         volt_real, volt_imag = turned[0], turned[1]
         left, right = weight_real[rows, :], weight_imag[rows, :]
         beam_real = half_dot(left, volt_real) - half_dot(right, volt_imag)
@@ -396,7 +454,8 @@
         binned = across(pool, high) + across(pool, middle) + across(pool, low)
         for part in range(owners):
             target = block * owners + part
-            piece = binned[:, part * beams_each : (part + 1) * beams_each]
+            wide = binned[:, part * beams_each : (part + 1) * beams_each]
+            piece = jnp.concatenate([wide[: samples // 2], wide[samples // 2 :]], axis=1)
 
             @pl.when(target == my_inp)
             def keep():
@@ -409,7 +468,7 @@
 
         return carry
 
-    lax.fori_loop(0, blocks, form, 0)
+    lax.fori_loop(0, form_blocks, form, 0)
 
     def take_power(k, carry):
         power_copy(other_inp(k), other_inp(k)).wait_recv()
@@ -417,15 +476,26 @@
 
     lax.fori_loop(1, inp_size, take_power, 0)
     for index in range(per_chan):
-        group = [power_in[index * FGROUPS + f] for f in range(FGROUPS)]
+        group = []
+        for f in range(FGROUPS):
+            piece = power_in[index * FGROUPS + f]
+            group += [piece[:, :beams_each], piece[:, beams_each:]]
         out_ref[index] = jnp.concatenate(group, axis=0).T
 
     def finish_inp(k, carry):
-        basis_copy(other_inp(k), my_inp).wait_send()
         power_copy(other_inp(k), my_inp).wait_send()
         return carry
 
     lax.fori_loop(1, inp_size, finish_inp, 0)
+    for offset in range(1, per_chan):
+        basis_cross(lax.rem(sub + offset, per_chan), my_inp).wait_send()
+
+    def finish_basis(index, carry):
+        slot = index // (FGROUPS - 1) * FGROUPS + place
+        basis_near(slot, peer(lax.rem(index, FGROUPS - 1) + 1)).wait_send()
+        return carry
+
+    lax.fori_loop(0, per_chan * (FGROUPS - 1), finish_basis, 0)
 
     def finish_volt(k, carry):
         volt_copy(other(k), me).wait_send()
@@ -456,17 +526,16 @@
         out_shape=jax.ShapeDtypeStruct(
             (per_chan, beams_each, FGROUPS * samples), jnp.float32
         ),
-        in_specs=[
-            pl.BlockSpec(memory_space=pl.ANY),
-            vmem,
-            vmem,
-            vmem,
-            pl.BlockSpec(memory_space=pltpu.SMEM),
-        ],
+        in_specs=[pl.BlockSpec(memory_space=pl.ANY)] * 5,
         out_specs=vmem,
         scratch_shapes=[
+            pltpu.VMEM((2, input_count), jnp.float32),
+            pltpu.VMEM((2, beam_count), jnp.float32),
+            pltpu.VMEM(basis.shape, jnp.float32),
+            pltpu.SMEM(rank_count.shape, jnp.int32),
             pltpu.VMEM((2, input_count, frames_dev), jnp.bfloat16),
-            pltpu.VMEM((inp_size, 2, ranks, basis_lanes), jnp.float32),
+            pltpu.VMEM((per_chan, ranks, 2 * basis_lanes), jnp.float32),
+            pltpu.VMEM((inp_size, ranks, 2 * basis_lanes), jnp.float32),
             row_block,
             row_block,
             row_block,
@@ -474,9 +543,10 @@
             pltpu.VMEM((2 * ranks, input_count), jnp.bfloat16),
             weight,
             weight,
-            pltpu.VMEM((inp_size, samples, beams_each), jnp.float32),
-            pltpu.VMEM((inp_size, samples, beams_each), jnp.float32),
+            pltpu.VMEM((inp_size, samples // 2, 2 * beams_each), jnp.float32),
+            pltpu.VMEM((inp_size, samples // 2, 2 * beams_each), jnp.float32),
             dma,
+            dma((4,)),
             dma((devices,)),
             dma((devices,)),
             dma((inp_size,)),
@@ -485,7 +555,7 @@
             dma((inp_size,)),
         ],
         compiler_params=pltpu.CompilerParams(
-            collective_id=0, has_side_effects=True, vmem_limit_bytes=40 * 1024 * 1024
+            collective_id=0, has_side_effects=True, vmem_limit_bytes=60 * 1024 * 1024
         ),
     )(voltages, positions.T, directions.T, basis, rank_count)
     return jnp.transpose(result, (1, 0, 2))
@@ -498,8 +568,8 @@
         voltages.shape[2] % 16 == 0
         and (voltages.shape[3] // FGROUPS) % 128 == 0
         and positions.shape[0] % ROWS == 0
-        and directions.shape[0] % ROWS == 0
-        and ROWS % beams_each == 0
+        and directions.shape[0] % FORM_ROWS == 0
+        and FORM_ROWS % beams_each == 0
     )
 
 

time: 55.7 us -> 49.7 us (0.89)
  local copies, waits for them, and re-layouts: 4.71 us -> 1.52 us
  Pallas kernels: 50.7 us -> 48 us
    unnamed x10 -> x0, local copies, waits for them, and re-layouts: 4.03 us -> none
    pallas_call x1, Pallas kernels: 50.7 us -> 48 us  [fused(): pl.pallas_call(functools.partial(fused_kernel, sizes), out_shape=jax.Shap...]
    transpose x1, local copies, waits for them, and re-layouts: 0.68 us -> 1.52 us  [fused(): return jnp.transpose(result, (1, 0, 2))]
where the time goes in v2:
time: 49.7 us; the launch traced here: 49.5 us
  Pallas kernels  48 us (97%)
  local copies, waits for them, and re-layouts  1.52 us (3%)
    pallas_call x1, Pallas kernels, fused(): pl.pallas_call(functools.partial(fused_kernel, sizes), out_shape=jax.Shap...  48 us
    transpose x1, local copies, waits for them, and re-layouts, fused(): return jnp.transpose(result, (1, 0, 2))  1.52 us

profile of v2, /device:TPU:0, one launch (start us, length us, event | category | flops | bytes accessed | tf_op | source)
XLA Modules:
  0.0 49.5 jit_solution(7284788528949354870)
XLA Ops:
  0.0 48.0 %shard_map.55 = f32[2,64,128]{2,1,0:T(8,128)} custom-call(bf16[2,4,32,2048]{3,2,1,0:T(8,128)(2,1)} %volt_ref.1, f32[2,1024]{1,0:T(2,128)} %bitcast.4, f32[2,1024]{1,0:T(2,128)} %bitcast.5, f32[2,2,16,64]{3,2,1,0:T(8,128)} %basis_hbm.1, s32[2]{0:T(128)} %rank_hbm.1), custom_call_target="tpu_custom_call" | custom-call | tf_op jit(solution)/shard_map/pallas_call | solution.py:524
  48.0 1.5 %copy.6 = f32[64,2,128]{2,1,0:T(2,128)} copy(f32[64,2,128]{2,0,1:T(8,128)} %bitcast.3) | data formatting | bytes 131072 | tf_op jit(solution)/shard_map/transpose | solution.py:561

commit v3 on v2

--- a/solution.py
+++ b/solution.py
@@ -13,6 +13,7 @@
 DS = 16
 ROWS = 128
 FORM_ROWS = 256
+FIRST_SENDS = 2
 MESH = pl.DeviceIdType.MESH
 
 
@@ -199,6 +200,8 @@
     ortho_real,
     ortho_imag,
     ortho_half,
+    steer_real,
+    steer_imag,
     weight_real,
     weight_imag,
     power_out,
@@ -339,16 +342,38 @@
         volt_copy(spread(k), me).start()
         return carry
 
-    lax.fori_loop(0, devices - half, send_volt, 0)
+    lax.fori_loop(0, FIRST_SENDS, send_volt, 0)
     for offset in range(1, per_chan):
         source = lax.rem(sub + offset, per_chan) * FGROUPS + place
         basis_near(source, place).wait_recv()
         pass_basis(source)
+    lax.fori_loop(FIRST_SENDS, devices - half, send_volt, 0)
     lax.fori_loop(devices - half + 1, devices, send_volt, 0)
     own = pltpu.make_async_copy(volt_block(me), turned_block(me), local_sem)
     own.start()
     for copy in staged[1:]:
         copy.wait()
+
+    channel = my_chan * per_chan + sub
+    frequency = 1.0 + 0.5 * channel.astype(jnp.float32) / (chan_size * per_chan)
+    sin_coefs, cos_coefs = turn_coefficients(input_count)
+
+    def steer(block, carry):
+        rows = pl.ds(pl.multiple_of(block * ROWS, ROWS), ROWS)
+        first = jnp.broadcast_to(dir_ref[0:1, rows], (ROWS, ROWS)).T
+        second = jnp.broadcast_to(dir_ref[1:2, rows], (ROWS, ROWS)).T
+        for piece in range(input_count // ROWS):
+            lanes = slice(piece * ROWS, (piece + 1) * ROWS)
+            turns = first * (pos_ref[0:1, lanes] * frequency) + second * (
+                pos_ref[1:2, lanes] * frequency
+            )
+            turns = turns - jnp.round(turns)
+            square = turns * turns
+            steer_real[rows, lanes] = horner(cos_coefs, square)
+            steer_imag[rows, lanes] = -turns * horner(sin_coefs, square)
+        return carry
+
+    lax.fori_loop(0, blocks, steer, 0)
 
     def take_basis(index, carry):
         slot = index // (FGROUPS - 1) * FGROUPS + peer(lax.rem(index, FGROUPS - 1) + 1)
@@ -394,38 +419,24 @@
         jnp.bfloat16
     )
 
-    channel = my_chan * per_chan + sub
-    frequency = 1.0 + 0.5 * channel.astype(jnp.float32) / (chan_size * per_chan)
-    sin_coefs, cos_coefs = turn_coefficients(input_count)
-
-    def weigh(block, carry):
-        rows = pl.ds(pl.multiple_of(block * ROWS, ROWS), ROWS)
-        first = jnp.broadcast_to(dir_ref[0:1, rows], (ROWS, ROWS)).T
-        second = jnp.broadcast_to(dir_ref[1:2, rows], (ROWS, ROWS)).T
-        reals, imags = [], []
-        for piece in range(input_count // ROWS):
-            lanes = slice(piece * ROWS, (piece + 1) * ROWS)
-            turns = first * (pos_ref[0:1, lanes] * frequency) + second * (
-                pos_ref[1:2, lanes] * frequency
-            )
-            turns = turns - jnp.round(turns)
-            square = turns * turns
-            reals.append(horner(cos_coefs, square))
-            imags.append(-turns * horner(sin_coefs, square))
-        steer_real = jnp.concatenate(reals, axis=1)
-        steer_imag = jnp.concatenate(imags, axis=1)
-        half = ortho_half[...]
-        from_real = across(steer_real.astype(jnp.bfloat16), half)
-        from_imag = across(steer_imag.astype(jnp.bfloat16), half)
+    def project(block, carry):
+        rows = pl.ds(pl.multiple_of(block * FORM_ROWS, FORM_ROWS), FORM_ROWS)
+        half_rows = ortho_half[...]
+        from_real = across(steer_real[rows, :].astype(jnp.bfloat16), half_rows)
+        from_imag = across(steer_imag[rows, :].astype(jnp.bfloat16), half_rows)
         along_real = from_real[:, :ranks] - from_imag[:, ranks:]
         along_imag = from_real[:, ranks:] + from_imag[:, :ranks]
         for_real = jnp.concatenate([along_real, along_imag], axis=1).astype(jnp.bfloat16)
         for_imag = jnp.concatenate([along_imag, -along_real], axis=1).astype(jnp.bfloat16)
-        weight_real[rows, :] = (steer_real - half_dot(for_real, half)).astype(jnp.bfloat16)
-        weight_imag[rows, :] = (steer_imag - half_dot(for_imag, half)).astype(jnp.bfloat16)
-        return carry
-
-    lax.fori_loop(0, blocks, weigh, 0)
+        weight_real[rows, :] = (steer_real[rows, :] - half_dot(for_real, half_rows)).astype(
+            jnp.bfloat16
+        )
+        weight_imag[rows, :] = (steer_imag[rows, :] - half_dot(for_imag, half_rows)).astype(
+            jnp.bfloat16
+        )
+        return carry
+
+    lax.fori_loop(0, form_blocks, project, 0)
 
     def take_volt(k, carry):
         volt_copy(other(k), other(k)).wait_recv()
@@ -440,7 +451,7 @@
     pool = jnp.where(inside, 1.0 / DS, 0.0).astype(jnp.bfloat16)
 
     def form(step, carry):
-        block = lax.rem(step + my_inp // owners, form_blocks)
+        block = lax.rem(step + my_inp // owners + 1, form_blocks)
         rows = pl.ds(pl.multiple_of(block * FORM_ROWS, FORM_ROWS), FORM_ROWS)
         volt_real, volt_imag = turned[0], turned[1]
         left, right = weight_real[rows, :], weight_imag[rows, :]
@@ -521,6 +532,7 @@
     dma = pltpu.SemaphoreType.DMA
     row_block = pltpu.VMEM((ranks, input_count), jnp.float32)
     weight = pltpu.VMEM((beam_count, input_count), jnp.bfloat16)
+    wave = pltpu.VMEM((beam_count, input_count), jnp.float32)
     result = pl.pallas_call(
         functools.partial(fused_kernel, sizes),
         out_shape=jax.ShapeDtypeStruct(
@@ -541,6 +553,8 @@
             row_block,
             row_block,
             pltpu.VMEM((2 * ranks, input_count), jnp.bfloat16),
+            wave,
+            wave,
             weight,
             weight,
             pltpu.VMEM((inp_size, samples // 2, 2 * beams_each), jnp.float32),

time: 49.7 us -> 43.8 us (0.88)
  Pallas kernels: 48 us -> 42 us
    pallas_call x1, Pallas kernels: 48 us -> 42 us  [fused(): pl.pallas_call(functools.partial(fused_kernel, sizes), out_shape=jax.Shap...]
where the time goes in v3:
time: 43.8 us; the launch traced here: 43.5 us
  Pallas kernels  42 us (96%)
  local copies, waits for them, and re-layouts  1.52 us (3%)
    pallas_call x1, Pallas kernels, fused(): pl.pallas_call(functools.partial(fused_kernel, sizes), out_shape=jax.Shap...  42 us
    transpose x1, local copies, waits for them, and re-layouts, fused(): return jnp.transpose(result, (1, 0, 2))  1.52 us

profile of v3, /device:TPU:0, one launch (start us, length us, event | category | flops | bytes accessed | tf_op | source)
XLA Modules:
  0.0 43.5 jit_solution(1395565790708745286)
XLA Ops:
  0.0 42.0 %shard_map.55 = f32[2,64,128]{2,1,0:T(8,128)} custom-call(bf16[2,4,32,2048]{3,2,1,0:T(8,128)(2,1)} %volt_ref.1, f32[2,1024]{1,0:T(2,128)} %bitcast.4, f32[2,1024]{1,0:T(2,128)} %bitcast.5, f32[2,2,16,64]{3,2,1,0:T(8,128)} %basis_hbm.1, s32[2]{0:T(128)} %rank_hbm.1), custom_call_target="tpu_custom_call" | custom-call | tf_op jit(solution)/shard_map/pallas_call | solution.py:536
  42.0 1.5 %copy.6 = f32[64,2,128]{2,1,0:T(2,128)} copy(f32[64,2,128]{2,0,1:T(8,128)} %bitcast.3) | data formatting | bytes 131072 | tf_op jit(solution)/shard_map/transpose | solution.py:575

commit v4 on v3

--- a/solution.py
+++ b/solution.py
@@ -438,12 +438,47 @@
 
     lax.fori_loop(0, form_blocks, project, 0)
 
-    def take_volt(k, carry):
-        volt_copy(other(k), other(k)).wait_recv()
-        return carry
-
-    own.wait()
-    lax.fori_loop(1, devices, take_volt, 0)
+    depth = half * local_inputs
+
+    def beams(rows, group):
+        start = pl.multiple_of(group * depth, depth)
+        left = weight_real[rows, pl.ds(start, depth)]
+        right = weight_imag[rows, pl.ds(start, depth)]
+        volt_real = turned[0, pl.ds(start, depth), :]
+        volt_imag = turned[1, pl.ds(start, depth), :]
+        return (
+            half_dot(left, volt_real) - half_dot(right, volt_imag),
+            half_dot(left, volt_imag) + half_dot(right, volt_real),
+        )
+
+    def take_group(offset):
+        group = lax.rem(sub + offset, per_chan)
+
+        def take_volt(k, carry):
+            source = group * half + lax.rem(me + k, half)
+            volt_copy(source, source).wait_recv()
+            return carry
+
+        if offset == 0:
+            own.wait()
+        lax.fori_loop(1 if offset == 0 else 0, half, take_volt, 0)
+        return group
+
+    for offset in range(per_chan - 1):
+        early = take_group(offset)
+
+        def form_early(block, carry):
+            rows = pl.ds(pl.multiple_of(block * FORM_ROWS, FORM_ROWS), FORM_ROWS)
+            beam_real, beam_imag = beams(rows, early)
+            if offset > 0:
+                beam_real = beam_real + steer_real[rows, :frames_dev]
+                beam_imag = beam_imag + steer_imag[rows, :frames_dev]
+            steer_real[rows, :frames_dev] = beam_real
+            steer_imag[rows, :frames_dev] = beam_imag
+            return carry
+
+        lax.fori_loop(0, form_blocks, form_early, 0)
+    last = take_group(per_chan - 1)
 
     sample_row = lax.broadcasted_iota(jnp.int32, (samples, frames_dev), 0)
     frame_column = lax.broadcasted_iota(jnp.int32, (samples, frames_dev), 1)
@@ -453,10 +488,10 @@
     def form(step, carry):
         block = lax.rem(step + my_inp // owners + 1, form_blocks)
         rows = pl.ds(pl.multiple_of(block * FORM_ROWS, FORM_ROWS), FORM_ROWS)
-        volt_real, volt_imag = turned[0], turned[1]
-        left, right = weight_real[rows, :], weight_imag[rows, :]
-        beam_real = half_dot(left, volt_real) - half_dot(right, volt_imag)
-        beam_imag = half_dot(left, volt_imag) + half_dot(right, volt_real)
+        beam_real, beam_imag = beams(rows, last)
+        if per_chan > 1:
+            beam_real = beam_real + steer_real[rows, :frames_dev]
+            beam_imag = beam_imag + steer_imag[rows, :frames_dev]
         power = beam_real * beam_real + beam_imag * beam_imag
         high = power.astype(jnp.bfloat16)
         rest = power - high.astype(jnp.float32)
@@ -583,6 +618,10 @@
         and (voltages.shape[3] // FGROUPS) % 128 == 0
         and positions.shape[0] % ROWS == 0
         and directions.shape[0] % FORM_ROWS == 0
+        and positions.shape[0] >= voltages.shape[3] // FGROUPS
+        and (inp_size * chan_size * voltages.shape[2]) == positions.shape[0]
+        and inp_size % FGROUPS == 0
+        and FGROUPS * chan_size * voltages.shape[2] % 128 == 0
         and FORM_ROWS % beams_each == 0
     )
 

time: 43.8 us -> 42.7 us (0.975)
  Pallas kernels: 42 us -> 40.9 us
    pallas_call x1, Pallas kernels: 42 us -> 40.9 us  [fused(): pl.pallas_call(functools.partial(fused_kernel, sizes), out_shape=jax.Shap...]
where the time goes in v4:
time: 42.7 us; the launch traced here: 42.5 us
  Pallas kernels  40.9 us (96%)
  local copies, waits for them, and re-layouts  1.52 us (4%)
    pallas_call x1, Pallas kernels, fused(): pl.pallas_call(functools.partial(fused_kernel, sizes), out_shape=jax.Shap...  40.9 us
    transpose x1, local copies, waits for them, and re-layouts, fused(): return jnp.transpose(result, (1, 0, 2))  1.52 us

profile of v4, /device:TPU:0, one launch (start us, length us, event | category | flops | bytes accessed | tf_op | source)
XLA Modules:
  0.0 42.5 jit_solution(16688943242795038666)
XLA Ops:
  0.0 40.9 %shard_map.55 = f32[2,64,128]{2,1,0:T(8,128)} custom-call(bf16[2,4,32,2048]{3,2,1,0:T(8,128)(2,1)} %volt_ref.1, f32[2,1024]{1,0:T(2,128)} %bitcast.4, f32[2,1024]{1,0:T(2,128)} %bitcast.5, f32[2,2,16,64]{3,2,1,0:T(8,128)} %basis_hbm.1, s32[2]{0:T(128)} %rank_hbm.1), custom_call_target="tpu_custom_call" | custom-call | tf_op jit(solution)/shard_map/pallas_call | solution.py:571
  41.0 1.5 %copy.6 = f32[64,2,128]{2,1,0:T(2,128)} copy(f32[64,2,128]{2,0,1:T(8,128)} %bitcast.3) | data formatting | bytes 131072 | tf_op jit(solution)/shard_map/transpose | solution.py:610

commit v5 on v4

--- a/solution.py
+++ b/solution.py
@@ -12,7 +12,7 @@
 FGROUPS = 8
 DS = 16
 ROWS = 128
-FORM_ROWS = 256
+FORM_ROWS = 512
 FIRST_SENDS = 2
 MESH = pl.DeviceIdType.MESH
 

time: 42.7 us -> 41.8 us (0.979)
  Pallas kernels: 40.9 us -> 40.1 us
    pallas_call x1, Pallas kernels: 40.9 us -> 40.1 us  [fused(): pl.pallas_call(functools.partial(fused_kernel, sizes), out_shape=jax.Shap...]
where the time goes in v5:
time: 41.8 us; the launch traced here: 41.6 us
  Pallas kernels  40.1 us (96%)
  local copies, waits for them, and re-layouts  1.52 us (4%)
    pallas_call x1, Pallas kernels, fused(): pl.pallas_call(functools.partial(fused_kernel, sizes), out_shape=jax.Shap...  40.1 us
    transpose x1, local copies, waits for them, and re-layouts, fused(): return jnp.transpose(result, (1, 0, 2))  1.52 us

profile of v5, /device:TPU:0, one launch (start us, length us, event | category | flops | bytes accessed | tf_op | source)
XLA Modules:
  0.0 41.6 jit_solution(7416631549256637581)
XLA Ops:
  0.0 40.1 %shard_map.55 = f32[2,64,128]{2,1,0:T(8,128)} custom-call(bf16[2,4,32,2048]{3,2,1,0:T(8,128)(2,1)} %volt_ref.1, f32[2,1024]{1,0:T(2,128)} %bitcast.4, f32[2,1024]{1,0:T(2,128)} %bitcast.5, f32[2,2,16,64]{3,2,1,0:T(8,128)} %basis_hbm.1, s32[2]{0:T(128)} %rank_hbm.1), custom_call_target="tpu_custom_call" | custom-call | tf_op jit(solution)/shard_map/pallas_call | solution.py:571
  40.1 1.5 %copy.6 = f32[64,2,128]{2,1,0:T(2,128)} copy(f32[64,2,128]{2,0,1:T(8,128)} %bitcast.3) | data formatting | bytes 131072 | tf_op jit(solution)/shard_map/transpose | solution.py:610
